TPU v7x, 128 devices: a whole 4x4x4 slice. The times are simulated.
128 devices in a mesh: fsdp: 64 (over y_lo, x, z, core), tp: 2 (over y_hi).
Axes of the slice: x: 4, y: 4 (y_hi: 2, y_lo: 2; y = y_hi * 2 + y_lo), z: 4, core: 2. Of those that a mesh axis runs over, the one named last changes fastest.
Arguments:
- activations: bfloat16 [25216, 768], P(('fsdp', 'tp')), may hold values from -24 to 24
- attn_gain: bfloat16 [2, 768], P(None, 'fsdp'), may hold values from 0.25 to 1.75
- qkv_weight: bfloat16 [2, 3, 768, 768], P(None, None, 'fsdp', 'tp'), may hold values from -0.21875 to 0.21875
- out_weight: bfloat16 [2, 768, 768], P(None, 'tp', 'fsdp'), may hold values from -0.875 to 0.875
- ffn_gain: bfloat16 [2, 768], P(None, 'fsdp'), may hold values from 0.25 to 1.75
- mlp_up: bfloat16 [768, 3072], P('fsdp', 'tp'), may hold values from -0.21875 to 0.21875
- mlp_down: bfloat16 [3072, 768], P('tp', 'fsdp'), may hold values from -0.109375 to 0.109375
- router: bfloat16 [768, 4], P('fsdp'), may hold values from -0.15625 to 0.15625
- expert_up: bfloat16 [4, 768, 3072], P(None, 'fsdp', 'tp'), may hold values from -0.21875 to 0.21875
- expert_down: bfloat16 [4, 3072, 768], P(None, 'tp', 'fsdp'), may hold values from -0.21875 to 0.21875
- routes: int32 [25216, 2], P('fsdp'), may hold values from 0 to 3, all different within a row; in each aligned block of 394 rows (0 to 393, 394 to 787, ...) at most 256 rows name the same one
- cotangent: bfloat16 [25216, 768], P(('fsdp', 'tp')), may hold values from -24 to 24
Outputs:
- result: bfloat16 [25216, 768], P(('fsdp', 'tp'))
- input_grad: float32 [25216, 768], P(('fsdp', 'tp'))
- attn_gain_grad: float32 [2, 768], P(None, 'fsdp')
- qkv_grad: float32 [2, 3, 768, 768], P(None, None, 'fsdp', 'tp')
- out_grad: float32 [2, 768, 768], P(None, 'tp', 'fsdp')
- ffn_gain_grad: float32 [2, 768], P(None, 'fsdp')
- mlp_up_grad: float32 [768, 3072], P('fsdp', 'tp')
- mlp_down_grad: float32 [3072, 768], P('tp', 'fsdp')
- router_grad: float32 [768, 4], P('fsdp')
- expert_up_grad: float32 [4, 768, 3072], P(None, 'fsdp', 'tp')
- expert_down_grad: float32 [4, 3072, 768], P(None, 'tp', 'fsdp')
Inputs may be any that keep to these rules, and one draw needn't show every extreme that they name: `routes`: each row names 2 different experts. In each aligned block of 394 rows (the images of one index of fsdp) no expert is named by more than 256 rows, a bound that some block reaches.
All inputs are finite; a program needn't handle non-finite values.
Results may differ from a plain program's by a relative error of at most 0.025.
Values may be sent and summed in bfloat16 or wider, within the bound.
A program may use at most 320 MiB of HBM per device.

v0:
```python
import jax
import jax.numpy as jnp
from jax import lax
from jax.sharding import PartitionSpec as P

HEAD = 64
SEQ = 197
CAP = 256


epsilon = 1e-06
precise = lax.Precision.HIGHEST


def in_blocks(x, dim, peers):
    lengths = x.shape
    tiles = x.reshape(*lengths[:dim], peers, lengths[dim] // peers, *lengths[dim + 1 :])
    return jnp.moveaxis(tiles, dim, 0)


def sum_at_owner(x, axis, dim):
    peers = lax.axis_size(axis)
    tiles = lax.all_to_all(in_blocks(x, dim, peers), axis, 0, 0, tiled=True)
    return jnp.sum(tiles.astype(jnp.float32), axis=0)


def laid_out(tiles, dim):
    tiles = jnp.moveaxis(tiles, 0, dim)
    lengths = tiles.shape
    return tiles.reshape(*lengths[:dim], lengths[dim] * lengths[dim + 1], *lengths[dim + 2 :])


def copy_for_each(x, axis):
    copies = jnp.broadcast_to(x, (lax.axis_size(axis), *x.shape))
    return lax.all_to_all(copies, axis, split_axis=0, concat_axis=0, tiled=True)


def gather_directly(x, axis, dim):
    return laid_out(copy_for_each(x, axis), dim)


def normed(values, norm_gain):
    centre = values - jnp.mean(values, axis=-1, keepdims=True)
    spread = jnp.mean(centre * centre, axis=-1, keepdims=True)
    return centre * lax.rsqrt(spread + epsilon) * norm_gain


def gelu_exact(values):
    return jax.nn.gelu(values, approximate=False)


def to_low(values):
    return values.astype(jnp.bfloat16)


def matmul(left, right):
    return jnp.dot(left, right, preferred_element_type=jnp.float32)


def spread_rows(residual, norm_gain):
    normal = normed(residual, norm_gain.astype(jnp.float32))
    return lax.all_gather(to_low(normal), "tp", axis=0, tiled=True)


def collect_rows(partial_value):
    return sum_at_owner(partial_value.astype(jnp.bfloat16), "tp", 0)


def spread_grad(grad_stream):
    return gather_directly(to_low(grad_stream), "tp", 0)


def collect_grad(partial_value):
    return sum_at_owner(partial_value.astype(jnp.bfloat16), "tp", 0)


def norm_back(residual, norm_gain, in_grad):
    unused, pullback = jax.vjp(normed, residual, norm_gain.astype(jnp.float32))
    return pullback(in_grad)


def fetch_attention(attn_gain, qkv_weight, out_weight, block_index):
    return (
        lax.all_gather(attn_gain[block_index], "fsdp", axis=0, tiled=True),
        lax.all_gather(qkv_weight[block_index], "fsdp", axis=1, tiled=True),
        lax.all_gather(out_weight[block_index], "fsdp", axis=1, tiled=True),
    )


def fetch_attention_again(attn_gain, qkv_weight, out_weight, block_index):
    return (
        lax.all_gather(attn_gain[block_index], "fsdp", axis=0, tiled=True),
        lax.all_gather(qkv_weight[block_index], "fsdp", axis=1, tiled=True),
        lax.all_gather(out_weight[block_index], "fsdp", axis=1, tiled=True),
    )


def return_attention(grads):
    return (
        lax.psum_scatter(grads[0], "fsdp", scatter_dimension=0, tiled=True),
        lax.psum_scatter(grads[1], "fsdp", scatter_dimension=1, tiled=True),
        lax.psum_scatter(grads[2], "fsdp", scatter_dimension=1, tiled=True),
    )


def attend_forward(residual, weights):
    norm_gain, qkv_matrix, out_matrix = weights
    inputs = spread_rows(residual, norm_gain)
    token_count = inputs.shape[0]
    image_count = token_count // SEQ
    head_count = qkv_matrix.shape[2] // HEAD
    projected = jnp.einsum("rd,cde->cre", inputs, qkv_matrix, preferred_element_type=jnp.float32)
    projected = to_low(projected).reshape(3, image_count, SEQ, head_count, HEAD)
    query_vectors, key_vectors, value_vectors = (projected[0], projected[1], projected[2])
    scores = jnp.einsum(
        "ishd,ithd->ihst", query_vectors, key_vectors, preferred_element_type=jnp.float32
    ) * HEAD ** (-0.5)
    row_peak = jnp.max(scores, axis=-1, keepdims=True)
    log_total = jnp.log(jnp.sum(jnp.exp(scores - row_peak), axis=-1, keepdims=True)) + row_peak
    attn_probs = jnp.exp(scores - log_total)
    mixed_heads = jnp.einsum(
        "ihst,ithd->ishd", to_low(attn_probs), value_vectors, preferred_element_type=jnp.float32
    )
    mixed_heads = to_low(mixed_heads).reshape(token_count, head_count * HEAD)
    branch = collect_rows(matmul(mixed_heads, out_matrix))
    saved = (residual, inputs, query_vectors, key_vectors, value_vectors, log_total, mixed_heads)
    return (residual + branch, saved)


def attend_backward(grad_stream, weights, saved):
    norm_gain, qkv_matrix, out_matrix = weights
    residual, inputs, query_vectors, key_vectors, value_vectors, log_total, mixed_heads = saved
    token_count = inputs.shape[0]
    image_count, head_count = (query_vectors.shape[0], query_vectors.shape[2])
    score_scale = HEAD ** (-0.5)
    branch_grad = spread_grad(grad_stream)
    out_matrix_grad = jnp.einsum(
        "rh,rd->hd", mixed_heads, branch_grad, preferred_element_type=jnp.float32
    )
    mixed_grad = jnp.einsum(
        "rd,hd->rh", branch_grad, out_matrix, preferred_element_type=jnp.float32
    )
    mixed_grad = to_low(mixed_grad).reshape(image_count, SEQ, head_count, HEAD)
    scores = (
        jnp.einsum(
            "ishd,ithd->ihst", query_vectors, key_vectors, preferred_element_type=jnp.float32
        )
        * score_scale
    )
    attn_probs = jnp.exp(scores - log_total)
    value_grad = to_low(
        jnp.einsum(
            "ihst,ishd->ithd", to_low(attn_probs), mixed_grad, preferred_element_type=jnp.float32
        )
    )
    prob_grad = jnp.einsum(
        "ishd,ithd->ihst", mixed_grad, value_vectors, preferred_element_type=jnp.float32
    )
    score_grad = to_low(
        attn_probs * (prob_grad - jnp.sum(attn_probs * prob_grad, axis=-1, keepdims=True))
    )
    query_grad = to_low(
        jnp.einsum("ihst,ithd->ishd", score_grad, key_vectors, preferred_element_type=jnp.float32)
        * score_scale
    )
    key_grad = to_low(
        jnp.einsum("ihst,ishd->ithd", score_grad, query_vectors, preferred_element_type=jnp.float32)
        * score_scale
    )
    stacked = jnp.stack([query_grad, key_grad, value_grad]).reshape(
        3, token_count, head_count * HEAD
    )
    qkv_matrix_grad = jnp.einsum("rd,cre->cde", inputs, stacked, preferred_element_type=jnp.float32)
    in_grad = collect_grad(
        jnp.einsum("cre,cde->rd", stacked, qkv_matrix, preferred_element_type=jnp.float32)
    )
    residual_grad, gain_grad = norm_back(residual, norm_gain, in_grad)
    return (grad_stream + residual_grad, (gain_grad, qkv_matrix_grad, out_matrix_grad))


def dense_forward(residual, weights):
    norm_gain, up_matrix, down_matrix = weights
    inputs = spread_rows(residual, norm_gain)
    hidden_pre = matmul(inputs, up_matrix)
    activated = to_low(gelu_exact(hidden_pre))
    branch = collect_rows(matmul(activated, down_matrix))
    return (residual + branch, (residual, inputs, hidden_pre, activated))


def dense_backward(grad_stream, weights, saved):
    norm_gain, up_matrix, down_matrix = weights
    residual, inputs, hidden_pre, activated = saved
    branch_grad = spread_grad(grad_stream)
    down_matrix_grad = jnp.einsum(
        "rf,rd->fd", activated, branch_grad, preferred_element_type=jnp.float32
    )
    act_grad = jnp.einsum("rd,fd->rf", branch_grad, down_matrix, preferred_element_type=jnp.float32)
    unused, pullback = jax.vjp(gelu_exact, hidden_pre)
    pre_grad = to_low(pullback(act_grad)[0])
    up_matrix_grad = jnp.einsum("rd,rf->df", inputs, pre_grad, preferred_element_type=jnp.float32)
    in_grad = collect_grad(
        jnp.einsum("rf,df->rd", pre_grad, up_matrix, preferred_element_type=jnp.float32)
    )
    residual_grad, gain_grad = norm_back(residual, norm_gain, in_grad)
    return (grad_stream + residual_grad, (gain_grad, up_matrix_grad, down_matrix_grad))


def route_table(route_block, expert_count, capacity):
    token_count = route_block.shape[0]
    labels = jnp.arange(expert_count, dtype=jnp.int32)
    chosen = jnp.sum((route_block[:, :, None] == labels[None, None, :]).astype(jnp.int32), axis=1)
    places = jnp.cumsum(chosen, axis=0) - 1
    places = jnp.where(chosen > 0, places, capacity)
    owners = jnp.broadcast_to(labels[None, :], (token_count, expert_count))
    sources = jnp.broadcast_to(
        jnp.arange(token_count, dtype=jnp.int32)[:, None], (token_count, expert_count)
    )
    table = (
        jnp.zeros((expert_count, capacity), jnp.int32).at[owners, places].set(sources, mode="drop")
    )
    counts = jnp.sum(chosen, axis=0)
    filled = (jnp.arange(capacity, dtype=jnp.int32)[None, :] < counts[:, None]).astype(jnp.float32)
    return (chosen.astype(jnp.float32), table, filled)


def expert_forward(residual, weights, route_block):
    norm_gain, router_matrix, up_stack, down_stack = weights
    expert_count = up_stack.shape[0]
    inputs = spread_rows(residual, norm_gain)
    token_count, width = inputs.shape
    router_probs = jax.nn.softmax(matmul(inputs, router_matrix), axis=-1)
    chosen, table, filled = route_table(route_block, expert_count, CAP)
    combine = router_probs * chosen
    slot_gates = jnp.take_along_axis(combine.T, table, axis=1) * filled
    slot_inputs = jnp.take(inputs, table, axis=0)
    hidden_pre = jnp.einsum(
        "ecd,edf->ecf", slot_inputs, up_stack, preferred_element_type=jnp.float32
    )
    activated = to_low(gelu_exact(hidden_pre))
    slot_out = jnp.einsum("ecf,efd->ecd", activated, down_stack, preferred_element_type=jnp.float32)
    weighted = (slot_gates[:, :, None] * slot_out).reshape(-1, width)
    partial_value = jnp.zeros((token_count, width), jnp.float32).at[table.reshape(-1)].add(weighted)
    branch = collect_rows(partial_value)
    saved = (
        residual,
        inputs,
        router_probs,
        chosen,
        table,
        filled,
        slot_gates,
        slot_inputs,
        hidden_pre,
        activated,
        slot_out,
    )
    return (residual + branch, saved)


def expert_backward(grad_stream, weights, saved):
    norm_gain, router_matrix, up_stack, down_stack = weights
    (
        residual,
        inputs,
        router_probs,
        chosen,
        table,
        filled,
        slot_gates,
        slot_inputs,
        hidden_pre,
        activated,
        slot_out,
    ) = saved
    expert_count = up_stack.shape[0]
    token_count, width = inputs.shape
    branch_grad = spread_grad(grad_stream)
    slot_grad = jnp.take(branch_grad, table, axis=0)
    gate_grad = (
        jnp.einsum("ecd,ecd->ec", slot_out, slot_grad, preferred_element_type=jnp.float32) * filled
    )
    out_slot_grad = to_low(slot_gates[:, :, None] * slot_grad)
    down_stack_grad = jnp.einsum(
        "ecf,ecd->efd", activated, out_slot_grad, preferred_element_type=jnp.float32
    )
    act_grad = jnp.einsum(
        "ecd,efd->ecf", out_slot_grad, down_stack, preferred_element_type=jnp.float32
    )
    unused, pullback = jax.vjp(gelu_exact, hidden_pre)
    pre_grad = to_low(pullback(act_grad)[0])
    up_stack_grad = jnp.einsum(
        "ecd,ecf->edf", slot_inputs, pre_grad, preferred_element_type=jnp.float32
    )
    slot_in_grad = jnp.einsum(
        "ecf,edf->ecd", pre_grad, up_stack, preferred_element_type=jnp.float32
    )
    labels = jnp.broadcast_to(jnp.arange(expert_count, dtype=jnp.int32)[:, None], table.shape)
    combine_grad = (
        jnp.zeros((token_count, expert_count), jnp.float32).at[table, labels].add(gate_grad)
    )
    probs_grad = combine_grad * chosen
    logit_grad = router_probs * (
        probs_grad - jnp.sum(router_probs * probs_grad, axis=-1, keepdims=True)
    )
    router_matrix_grad = jnp.einsum(
        "rd,re->de", inputs.astype(jnp.float32), logit_grad, precision=precise
    )
    in_grad = (
        jnp.zeros((token_count, width), jnp.float32)
        .at[table.reshape(-1)]
        .add(slot_in_grad.reshape(-1, width))
    )
    in_grad = in_grad + jnp.einsum(
        "re,de->rd", logit_grad, router_matrix.astype(jnp.float32), precision=precise
    )
    in_grad = collect_grad(in_grad)
    residual_grad, gain_grad = norm_back(residual, norm_gain, in_grad)
    return (
        grad_stream + residual_grad,
        (gain_grad, router_matrix_grad, up_stack_grad, down_stack_grad),
    )


def body(
    activations,
    attn_gain,
    qkv_weight,
    out_weight,
    ffn_gain,
    mlp_up,
    mlp_down,
    router,
    expert_up,
    expert_down,
    routes,
    cotangent,
):
    first_attention = fetch_attention(attn_gain, qkv_weight, out_weight, 0)
    residual = activations.astype(jnp.float32)
    residual, saved_first = attend_forward(residual, first_attention)
    dense_set = (
        lax.all_gather(ffn_gain[0], "fsdp", axis=0, tiled=True),
        lax.all_gather(mlp_up, "fsdp", axis=0, tiled=True),
        lax.all_gather(mlp_down, "fsdp", axis=1, tiled=True),
    )
    residual, saved_dense = dense_forward(residual, dense_set)
    second_attention = fetch_attention(attn_gain, qkv_weight, out_weight, 1)
    residual, saved_second = attend_forward(residual, second_attention)
    expert_set = (
        lax.all_gather(ffn_gain[1], "fsdp", axis=0, tiled=True),
        lax.all_gather(router, "fsdp", axis=0, tiled=True),
        lax.all_gather(expert_up, "fsdp", axis=1, tiled=True),
        lax.all_gather(expert_down, "fsdp", axis=2, tiled=True),
    )
    residual, saved_experts = expert_forward(residual, expert_set, routes)
    result = to_low(residual)
    grad_stream = cotangent.astype(jnp.float32)
    expert_set = (
        lax.all_gather(ffn_gain[1], "fsdp", axis=0, tiled=True),
        lax.all_gather(router, "fsdp", axis=0, tiled=True),
        lax.all_gather(expert_up, "fsdp", axis=1, tiled=True),
        lax.all_gather(expert_down, "fsdp", axis=2, tiled=True),
    )
    grad_stream, expert_grads = expert_backward(grad_stream, expert_set, saved_experts)
    expert_grads = (
        lax.psum_scatter(expert_grads[0], "fsdp", scatter_dimension=0, tiled=True),
        lax.psum_scatter(expert_grads[1], "fsdp", scatter_dimension=0, tiled=True),
        lax.psum_scatter(expert_grads[2], "fsdp", scatter_dimension=1, tiled=True),
        lax.psum_scatter(expert_grads[3], "fsdp", scatter_dimension=2, tiled=True),
    )
    second_attention = fetch_attention_again(attn_gain, qkv_weight, out_weight, 1)
    grad_stream, second_grads = attend_backward(grad_stream, second_attention, saved_second)
    second_grads = return_attention(second_grads)
    dense_set = (
        lax.all_gather(ffn_gain[0], "fsdp", axis=0, tiled=True),
        lax.all_gather(mlp_up, "fsdp", axis=0, tiled=True),
        lax.all_gather(mlp_down, "fsdp", axis=1, tiled=True),
    )
    grad_stream, dense_grads = dense_backward(grad_stream, dense_set, saved_dense)
    dense_grads = (
        lax.psum_scatter(dense_grads[0], "fsdp", scatter_dimension=0, tiled=True),
        lax.psum_scatter(dense_grads[1], "fsdp", scatter_dimension=0, tiled=True),
        lax.psum_scatter(dense_grads[2], "fsdp", scatter_dimension=1, tiled=True),
    )
    first_attention = fetch_attention_again(attn_gain, qkv_weight, out_weight, 0)
    grad_stream, first_grads = attend_backward(grad_stream, first_attention, saved_first)
    first_grads = return_attention(first_grads)
    attn_gain_grad = jnp.stack([first_grads[0], second_grads[0]])
    ffn_gain_grad = jnp.stack([dense_grads[0], expert_grads[0]])
    attn_gain_grad, ffn_gain_grad, router_grad = lax.psum(
        (attn_gain_grad, ffn_gain_grad, expert_grads[1]), "tp"
    )
    qkv_grad = jnp.stack([first_grads[1], second_grads[1]])
    out_grad = jnp.stack([first_grads[2], second_grads[2]])
    return (
        result,
        grad_stream,
        attn_gain_grad,
        qkv_grad,
        out_grad,
        ffn_gain_grad,
        dense_grads[1],
        dense_grads[2],
        router_grad,
        expert_grads[2],
        expert_grads[3],
    )


def solution(mesh):
    placed = (
        P(("fsdp", "tp"), None),
        P(None, "fsdp"),
        P(None, None, "fsdp", "tp"),
        P(None, "tp", "fsdp"),
        P(None, "fsdp"),
        P("fsdp", "tp"),
        P("tp", "fsdp"),
        P("fsdp", None),
        P(None, "fsdp", "tp"),
        P(None, "tp", "fsdp"),
        P("fsdp", None),
        P(("fsdp", "tp"), None),
    )
    return jax.shard_map(
        body,
        mesh=mesh,
        in_specs=placed,
        out_specs=(
            P(("fsdp", "tp"), None),
            P(("fsdp", "tp"), None),
            P(None, "fsdp"),
            P(None, None, "fsdp", "tp"),
            P(None, "tp", "fsdp"),
            P(None, "fsdp"),
            P("fsdp", "tp"),
            P("tp", "fsdp"),
            P("fsdp", None),
            P(None, "fsdp", "tp"),
            P(None, "tp", "fsdp"),
        ),
        check_vma=False,
    )
```

profile of v0, /device:TPU:0, one launch (start us, length us, event | category | flops | bytes accessed | tf_op | source)
XLA Modules:
  0.0 1711.0 jit_solution(4003756410644233586)
XLA Ops:
  19.0 147.5 %all-reduce.25 = (bf16[768]{0:T(1024)(128)(2,1)S(1)}, bf16[768]{0:T(1024)(128)(2,1)S(1)}, bf16[768]{0:T(1024)(128)(2,1)S(1)}, bf16[768]{0:T(1024)(128)(2,1)S(1)}) all-reduce(bf16[768]{0:T(1024)(128)(2,1)S(1)} %dynamic-update-slice, bf16[768]{0:T(1024)(128)(2,1)S(1)} %dynamic-update-slice.1, ...), channel_id=2, replica_groups=mesh['fsdp'=64,'tp'=2] {'fsdp'}, use_global_device_ids=true, to_apply=%add.1 | all-reduce | flops 3072 | bytes 12288
  171.9 8.8 scatter_custom_fusion.2
  180.9 9.0 all-gather.8
  190.1 79.4 %all-gather.6 = bf16[1,384,768]{1,0,2:T(2,128)(2,1)S(1)} all-gather(bf16[1,384,12]{1,0,2:T(2,128)(2,1)S(1)} %get-tuple-element.123), channel_id=8, replica_groups=mesh['fsdp'=64,'tp'=2] {'fsdp'}, dimensions={2}, use_global_device_ids=true | all-gather | bytes 599040 | tf_op jit(solution)/shard_map/all_gather | solution.py:86
  272.5 81.6 %all-gather.2 = bf16[1,384,768]{1,0,2:T(2,128)(2,1)S(1)} all-gather(bf16[1,384,12]{1,0,2:T(2,128)(2,1)S(1)} %get-tuple-element.124), channel_id=4, replica_groups=mesh['fsdp'=64,'tp'=2] {'fsdp'}, dimensions={2}, use_global_device_ids=true | all-gather | bytes 599040 | tf_op jit(solution)/shard_map/all_gather | solution.py:86
  369.8 10.9 all-to-all-done
  381.4 10.6 all-gather.9
  396.6 5.3 reshape.449
  401.8 8.7 multiply_convert_fusion.3
  417.3 9.1 all-to-all-done.1
  432.2 14.2 all-gather.12
  460.7 79.2 %all-gather.14 = bf16[64,12,4]{1,2,0:T(4,128)(2,1)S(1)} all-gather(bf16[1,12,4]{1,2,0:T(4,128)(2,1)S(1)} %bitcast.244), channel_id=1, replica_groups=mesh['fsdp'=64,'tp'=2] {'fsdp'}, dimensions={0}, use_global_device_ids=true | all-gather | bytes 6240 | tf_op jit(solution)/shard_map/all_gather | solution.py:351
  547.6 13.0 all-gather.13
  561.9 5.2 gather_fusion.1
  567.4 9.1 gather_fusion
  579.3 8.1 fusion.39
  590.0 15.1 multiply_convert_fusion
  605.2 57.5 %all-gather.24.cloned.1.call-done = bf16[4,1536,768]{1,0,2:T(4,128)(2,1)} async-done(((bf16[4,1536,12]{1,0,2:T(4,128)(2,1)}), bf16[4,1536,768]{1,0,2:T(4,128)(2,1)}) %all-gather.24.cloned.1.call-update) | async-done | bytes 9437200 | tf_op jit(solution)/shard_map/all_gather | solution.py:353
  662.6 10.1 fusion.18
  672.8 7.8 scatter_custom_fusion.3
  681.5 11.3 add_convert_fusion
  692.8 5.1 fusion.8
  697.9 8.5 scatter_fusion
  707.4 4.7 all-to-all-start.5
  712.1 8.4 scatter_custom_fusion
  728.4 8.7 all-to-all-done.3
  738.9 12.5 all_to_all.60
  771.3 11.3 all_to_all.61
  788.4 11.2 fusion.81
  799.7 5.0 add_convert_fusion.1
  807.9 4.8 all-to-all-start.9
  817.2 23.4 %copy.256 = f32[4,1536,768]{1,0,2:T(4,128)} copy(f32[4,1536,768]{1,2,0:T(8,128)} %fusion.81) | data formatting | bytes 37748736 | tf_op jit(solution)/shard_map/ecf,ecd->efd/dot_general | solution.py:283
  840.6 30.7 %copy.254 = f32[4,768,1536]{2,0,1:T(4,128)} copy(f32[4,768,1536]{2,1,0:T(8,128)S(1)} %fusion.52) | data formatting | bytes 37748736 | tf_op jit(solution)/shard_map/ecd,ecf->edf/dot_general | solution.py:291
  874.4 4.8 all-to-all-start.10
  912.0 5.0 fusion.156
  921.2 191.4 %fusion.137 = (f32[384,16]{0,1:T(8,128)S(1)}, f32[384,16]{0,1:T(8,128)S(1)}, f32[16,1536]{1,0:T(8,128)S(1)}, f32[1536,16]{0,1:T(8,128)S(1)}) fusion(f32[384,768]{0,1:T(8,128)S(1)} %fusion.155, f32[384,768]{0,1:T(8,128)S(1)} %fusion.154, f32[768,1536]{1,0:T(8,128)} %fusion.156, f32[1536,768]{0,1:T(8,128)} %fusion.157), kind=kCustom, calls=%all-reduce-scatter.4 | all-reduce-scatter fusion | flops 3932161 | bytes 12042752
  1113.9 4.9 collective-permute-start.15
  1118.8 5.6 collective-permute-start.31
  1129.7 5.1 collective-permute-start.25
  1139.2 5.2 collective-permute-start.22
  1147.9 5.3 collective-permute-start.19
  1221.7 5.1 collective-permute-start.37
  1230.8 4.7 all-to-all-start.11
  1282.2 12.5 concatenate.15
  1311.5 26.2 %concatenate.16 = f32[1536,268]{0,1:T(8,128)} concatenate(f32[1536,12]{0,1:T(8,128)S(1)} %collective-permute-done.63, f32[1536,16]{0,1:T(8,128)} %copy-done.69, f32[1536,16]{0,1:T(8,128)} %copy-done.70, f32[1536,16]{0,1:T(8,128)} %copy-done.71, f32[1536,16]{0,1:T(8,128)} %copy-done.72, f32[1536,16]{0,1:T(8,128)} %copy-done.74, f32[1536,16]{0,1:T(8,128)} %collective-permute-done.57, ...), dimensions={1} | concatenate | bytes 3293184
  1340.2 277.2 %all-reduce.22 = (f32[768]{0:T(1024)S(1)}, f32[768]{0:T(1024)S(1)}, f32[768]{0:T(1024)S(1)}, f32[768]{0:T(1024)S(1)}, f32[768,4]{0,1:T(4,128)S(1)}) all-reduce(f32[768]{0:T(1024)S(1)} %get-tuple-element.62, f32[768]{0:T(1024)S(1)} %get-tuple-element.64, ...), channel_id=11, replica_groups=mesh['fsdp'=64,'tp'=2] {'fsdp'}, use_global_device_ids=true, to_apply=%region_44.46.clone | all-reduce | flops 6144 | bytes 49152
  1617.7 8.1 all-reduce.24
  1626.9 71.9 %all-reduce.29.cloned.1.call-done = (f32[3,768,384]{2,0,1:T(4,128)}, f32[3,768,384]{2,0,1:T(4,128)}, f32[4,768,1536]{2,0,1:T(4,128)}, f32[4,1536,768]{1,0,2:T(4,128)}) async-done(((f32[3,768,384]{2,0,1:T(4,128)}, f32[3,768,384]{2,0,1:T(4,128)}, f32[4,768,1536]{2,0,1:T(4,128)}, f32[4,1536,768]{1,0,2:T(4,128)}), (f32[3,768,384]{2,0,1:T(4,128)}, f32[3,768,384]{2,0,1:T(4,128)}, f32[4,768,1536]{2,0,1:T(4,128)}, ...) | async-done | bytes 44826640
  (601 shorter events, 323.2 us)
Async XLA Ops:
  7.2 348.7 %all-gather.26.cloned.1.call-start = ((), (), s32[]{:S(2)}) async-start(), calls=%async_computation.14 | async-start | bytes 2396160 | tf_op jit(solution)/shard_map/all_gather | solution.py:85
  8.9 384.0 %all-gather.30.cloned.1.call-start = ((), (), s32[]{:S(2)}) async-start(), calls=%async_computation.16 | async-start | bytes 3194880 | tf_op jit(solution)/shard_map/all_gather | solution.py:343
  9.6 386.9 %all-gather.32.cloned.1.call-start = ((), (), s32[]{:S(2)}) async-start(), calls=%async_computation.17 | async-start | bytes 3194880 | tf_op jit(solution)/shard_map/all_gather | solution.py:344
  10.4 436.2 %all-gather.28.cloned.1.call-start = ((), (), s32[]{:S(2)}) async-start(), calls=%async_computation.15 | async-start | bytes 2396160 | tf_op jit(solution)/shard_map/all_gather | solution.py:85
  11.1 568.2 %all-gather.22.cloned.1.call-start = ((), (), s32[]{:S(2)}) async-start(), calls=%async_computation.12 | async-start | bytes 9584640 | tf_op jit(solution)/shard_map/all_gather | solution.py:352
  11.7 651.0 %all-gather.24.cloned.1.call-start = ((), (), s32[]{:S(2)}) async-start(), calls=%async_computation.13 | async-start | bytes 9584640 | tf_op jit(solution)/shard_map/all_gather | solution.py:353
  365.7 15.0 all-to-all-start
  413.7 12.7 all-to-all-start.1
  427.3 29.1 %all-to-all-start.4 = ((bf16[2,197,768]{2,1,0:T(8,128)(2,1)}), bf16[2,197,768]{2,1,0:T(8,128)(2,1)}, u32[]{:S(2)}, u32[]{:S(2)}) async-start(bf16[2,197,768]{2,1,0:T(8,128)(2,1)} %broadcast_in_dim.58), calls=%async_computation.4 | async-start | bytes 1228800 | tf_op jit(solution)/shard_map/all_to_all | solution.py:35
  456.4 89.0 %all-to-all-start.2 = ((bf16[2,197,768]{2,1,0:T(8,128)(2,1)}), bf16[2,197,768]{2,1,0:T(8,128)(2,1)}, u32[]{:S(2)}, u32[]{:S(2)}) async-start(bf16[2,197,768]{2,1,0:T(8,128)(2,1)} %reshape.337), calls=%async_computation.2 | async-start | bytes 1228800 | tf_op jit(solution)/shard_map/all_to_all | solution.py:23
  707.4 15.8 all-to-all-start.5
  723.3 13.8 all-to-all-start.3
  784.9 14.7 all-to-all-start.8
  807.9 63.4 %all-to-all-start.9 = ((bf16[2,197,768]{2,1,0:T(8,128)(2,1)}), bf16[2,197,768]{2,1,0:T(8,128)(2,1)S(1)}, u32[]{:S(2)}, u32[]{:S(2)}) async-start(bf16[2,197,768]{2,1,0:T(8,128)(2,1)} %reshape.351), calls=%async_computation.9 | async-start | bytes 1228800 | tf_op jit(solution)/shard_map/all_to_all | solution.py:23
  874.4 13.5 all-to-all-start.10
  879.2 819.6 %all-reduce.29.cloned.1.call-start = ((), (), s32[]{:S(2)}) async-start(), calls=%async_computation.18 | async-start | bytes 94371840
  1112.6 17.1 collective-permute-start.30
  1113.9 13.1 collective-permute-start.15
  1128.4 16.0 collective-permute-start.26
  1129.7 16.0 collective-permute-start.25
  1134.8 13.1 collective-permute-start.24
  1137.9 15.3 collective-permute-start.23
  1139.2 15.3 collective-permute-start.22
  1144.4 12.3 collective-permute-start.21
  1145.7 14.2 collective-permute-start.20
  1147.9 14.2 collective-permute-start.19
  1178.3 29.3 %collective-permute-start.63 = (f32[1536,12]{0,1:T(8,128)S(1)}, f32[1536,12]{0,1:T(8,128)S(1)}, u32[]{:S(2)}, u32[]{:S(2)}) collective-permute-start(f32[1536,12]{0,1:T(8,128)S(1)} %slice.99), channel_id=1, source_target_pairs={{0,32},{2,34},{4,36},{6,38},{8,40},{10,42},{12,44},{14,46},{16,48}... | collective-permute-start | bytes 221192
  1179.9 31.0 %collective-permute-start.47 = (f32[12,1536]{1,0:T(8,128)S(1)}, f32[12,1536]{1,0:T(8,128)S(1)}, u32[]{:S(2)}, u32[]{:S(2)}) collective-permute-start(f32[12,1536]{1,0:T(8,128)S(1)} %slice.98), channel_id=1, source_target_pairs={{0,32},{2,34},{4,36},{6,38},{8,40},{10,42},{12,44},{14,46},{16,48}... | collective-permute-start | bytes 221192
  1200.1 12.4 collective-permute-start.46
  1212.6 28.2 %collective-permute-start.41 = (f32[16,1536]{1,0:T(8,128)S(1)}, f32[16,1536]{1,0:T(8,128)S(1)}, u32[]{:S(2)}, u32[]{:S(2)}) collective-permute-start(f32[16,1536]{1,0:T(8,128)S(1)} %get-tuple-element.90), channel_id=1, source_target_pairs={{0,20},{2,22},{4,24},{6,26},{8,28},{10,30},{12,32},{14,34},{16,36}... | collective-permute-start | bytes 294920
  1214.5 27.5 %collective-permute-start.40 = (f32[16,1536]{1,0:T(8,128)S(1)}, f32[16,1536]{1,0:T(8,128)S(1)}, u32[]{:S(2)}, u32[]{:S(2)}) collective-permute-start(f32[16,1536]{1,0:T(8,128)S(1)} %get-tuple-element.90), channel_id=1, source_target_pairs={{0,18},{2,20},{4,22},{6,24},{8,26},{10,28},{12,30},{14,32},{16,34}... | collective-permute-start | bytes 294920
  1216.7 29.7 %collective-permute-start.39 = (f32[16,1536]{1,0:T(8,128)S(1)}, f32[16,1536]{1,0:T(8,128)S(1)}, u32[]{:S(2)}, u32[]{:S(2)}) collective-permute-start(f32[16,1536]{1,0:T(8,128)S(1)} %get-tuple-element.90), channel_id=1, source_target_pairs={{0,16},{2,18},{4,20},{6,22},{8,24},{10,26},{12,28},{14,30},{16,32}... | collective-permute-start | bytes 294920
  1218.1 29.7 %collective-permute-start.38 = (f32[16,1536]{1,0:T(8,128)S(1)}, f32[16,1536]{1,0:T(8,128)S(1)}, u32[]{:S(2)}, u32[]{:S(2)}) collective-permute-start(f32[16,1536]{1,0:T(8,128)S(1)} %get-tuple-element.90), channel_id=1, source_target_pairs={{0,14},{2,16},{4,18},{6,20},{8,22},{10,24},{12,26},{14,28},{16,30}... | collective-permute-start | bytes 294920
  1221.7 29.4 %collective-permute-start.37 = (f32[16,1536]{1,0:T(8,128)S(1)}, f32[16,1536]{1,0:T(8,128)S(1)}, u32[]{:S(2)}, u32[]{:S(2)}) collective-permute-start(f32[16,1536]{1,0:T(8,128)S(1)} %get-tuple-element.90), channel_id=1, source_target_pairs={{0,12},{2,14},{4,16},{6,18},{8,20},{10,22},{12,24},{14,26},{16,28}... | collective-permute-start | bytes 294920
  1230.8 108.5 %all-to-all-start.11 = ((bf16[2,197,768]{2,1,0:T(8,128)(2,1)}), bf16[2,197,768]{2,1,0:T(8,128)(2,1)S(1)}, u32[]{:S(2)}, u32[]{:S(2)}) async-start(bf16[2,197,768]{2,1,0:T(8,128)(2,1)} %reshape.354), calls=%async_computation.11 | async-start | bytes 1228800 | tf_op jit(solution)/shard_map/all_to_all | solution.py:23
  1240.8 13.0 collective-permute-start.36
  1242.1 15.7 collective-permute-start.35
  1246.5 14.3 collective-permute-start.34
  1247.8 14.3 collective-permute-start.33
  1251.1 12.9 collective-permute-start.32
  1262.2 12.8 collective-permute-start.59
  1264.1 14.9 collective-permute-start.58
  1265.6 29.1 %collective-permute-start.57 = (f32[1536,16]{0,1:T(8,128)S(1)}, f32[1536,16]{0,1:T(8,128)}, u32[]{:S(2)}, u32[]{:S(2)}) collective-permute-start(f32[1536,16]{0,1:T(8,128)S(1)} %get-tuple-element.91), channel_id=1, source_target_pairs={{0,20},{2,22},{4,24},{6,26},{8,28},{10,30},{12,32},{14,34},{16,36}... | collective-permute-start | bytes 294920
  1269.6 28.8 %collective-permute-start.56 = (f32[1536,16]{0,1:T(8,128)S(1)}, f32[1536,16]{0,1:T(8,128)}, u32[]{:S(2)}, u32[]{:S(2)}) collective-permute-start(f32[1536,16]{0,1:T(8,128)S(1)} %get-tuple-element.91), channel_id=1, source_target_pairs={{0,18},{2,20},{4,22},{6,24},{8,26},{10,28},{12,30},{14,32},{16,34}... | collective-permute-start | bytes 294920
  1272.5 27.9 %collective-permute-start.55 = (f32[1536,16]{0,1:T(8,128)S(1)}, f32[1536,16]{0,1:T(8,128)}, u32[]{:S(2)}, u32[]{:S(2)}) collective-permute-start(f32[1536,16]{0,1:T(8,128)S(1)} %get-tuple-element.91), channel_id=1, source_target_pairs={{0,16},{2,18},{4,20},{6,22},{8,24},{10,26},{12,28},{14,30},{16,32}... | collective-permute-start | bytes 294920
  1275.0 28.8 %collective-permute-start.54 = (f32[1536,16]{0,1:T(8,128)S(1)}, f32[1536,16]{0,1:T(8,128)}, u32[]{:S(2)}, u32[]{:S(2)}) collective-permute-start(f32[1536,16]{0,1:T(8,128)S(1)} %get-tuple-element.91), channel_id=1, source_target_pairs={{0,14},{2,16},{4,18},{6,20},{8,22},{10,24},{12,26},{14,28},{16,30}... | collective-permute-start | bytes 294920
  1279.0 28.2 %collective-permute-start.53 = (f32[1536,16]{0,1:T(8,128)S(1)}, f32[1536,16]{0,1:T(8,128)}, u32[]{:S(2)}, u32[]{:S(2)}) collective-permute-start(f32[1536,16]{0,1:T(8,128)S(1)} %get-tuple-element.91), channel_id=1, source_target_pairs={{0,12},{2,14},{4,16},{6,18},{8,20},{10,22},{12,24},{14,26},{16,28}... | collective-permute-start | bytes 294920
  1294.8 14.6 collective-permute-start.52
  (138 other events, 4067.4 us)
Sparse Core Ops, SparseCore 0:
  10.3 106.6 all-gather.25
  118.7 104.2 all-gather.29
  224.8 104.0 all-gather.31
  331.0 103.5 all-gather.27
  436.1 112.9 all-gather.21
  550.7 111.9 all-gather.23
  910.3 788.4 all-reduce.28
where the time goes:
time: 1720 us; the launch traced here: 1710 us
  blocking collectives  935 us (54%)
  local copies, waits for them, and re-layouts  214 us (12%)
  starting transfers between devices  208 us (12%)
  waiting for transfers between devices  166 us (10%)
  matrix products  108 us (6%)
  other arithmetic  60.1 us (3%)
  between operations  19.4 us (1%)
    unnamed x3, blocking collectives  616 us
    unnamed x65, starting transfers between devices  166 us
    all_gather x2, blocking collectives, fetch_attention(): lax.all_gather(out_weight[block_index], 'fsdp', axis=1, tiled=True)  161 us
    unnamed x257, local copies, waits for them, and re-layouts  87.7 us
    all_gather x1, blocking collectives, body(): lax.all_gather(router, 'fsdp', axis=0, tiled=True)  79.2 us
    unnamed x72, waiting for transfers between devices  76.7 us
    all_gather x1, waiting for transfers between devices, body(): lax.all_gather(expert_down, 'fsdp', axis=2, tiled=True)  57.5 us
    all_gather x4, blocking collectives, spread_rows(): return lax.all_gather(to_low(normal), 'tp', axis=0, tiled=True)  46.8 us
  transfers between devices with their start and end apart: 81, of which 8 were waited for; matrix products, arithmetic and copies ran while one was open for 27% of the time, Pallas kernels for 0%

commit v1 on v0

v1 whole, which is shorter than its diff:
```python
import functools
import itertools

import jax
import jax.numpy as jnp
from jax import lax
from jax.experimental import pallas as pl
from jax.experimental.pallas import tpu as pltpu
from jax.sharding import PartitionSpec as P

HEAD = 64
SEQ = 197
D = 768
HALF = 1536
SMALL = 128
WIDE = HALF + SMALL
MESH = pl.DeviceIdType.MESH
GROUPS = [[4 * k + j for j in range(4)] for k in range(16)]

epsilon = 1e-06
precise = lax.Precision.HIGHEST

ORDERS = (("x", "y", "z"), ("y", "z", "x"), ("z", "x", "y"))
WIDTHS = (WIDE, HALF, HALF)


def to_low(values):
    return values.astype(jnp.bfloat16)


def coordinates():
    f, t = lax.axis_index("fsdp"), lax.axis_index("tp")
    return {
        "x": lax.rem(lax.div(f, 8), 4),
        "y": 2 * t + lax.div(f, 32),
        "z": lax.rem(lax.div(f, 2), 4),
        "c": lax.rem(f, 2),
    }


def device_at(place):
    y = place["y"]
    f = ((lax.rem(y, 2) * 4 + place["x"]) * 4 + place["z"]) * 2 + place["c"]
    return (f, lax.div(y, 2))


def moved(place, axis, steps):
    return {**place, axis: lax.rem(place[axis] + steps + 4, 4)}


def greet(place):
    others = [device_at(moved(place, a, s)) for a in "xyz" for s in (1, -1)]
    others.append(device_at({**place, "c": 1 - place["c"]}))
    barrier = pltpu.get_barrier_semaphore()
    for other in others:
        pl.semaphore_signal(barrier, inc=1, device_id=other, device_id_type=MESH)
    pl.semaphore_wait(barrier, len(others))


def cube(where, whole):
    every = slice(None)
    y = (every, every) if "y" in whole else (lax.div(where["y"], 2), lax.rem(where["y"], 2))
    z = (every, every) if "z" in whole else (lax.rem(where["z"], 2), lax.div(where["z"], 2))
    x = every if "x" in whole else where["x"]
    return (z[0], y[0], y[1], x, z[1])


def halves(width):
    first = (width // 256) * 128
    if width - first > first:
        first = width - first
    return (slice(0, first), slice(first, width))


def gather_kernel(*refs):
    n = len(WIDTHS)
    shards, wholes = refs[:n], refs[n : 2 * n]
    send_sem, recv_sem, send_pair, recv_pair, own_sem = refs[2 * n :]
    me = coordinates()
    sibling = {**me, "c": 1 - me["c"]}
    greet(me)

    def block(m, p, where, whole, cols=slice(None)):
        z_lo, t, y_lo, x, z_hi = cube(where, whole)
        return wholes[m].at[z_lo, me["c"], t, y_lo, x, z_hi, pl.ds(16 * p, 16), cols]

    pending = []
    pair_count = [0] * n

    def pair_send(src, dst, m):
        slot = pair_count[m]
        pair_count[m] += 1
        copy = pltpu.make_async_remote_copy(
            src_ref=src,
            dst_ref=dst,
            send_sem=send_pair.at[m, slot],
            recv_sem=recv_pair.at[m, slot],
            device_id=device_at(sibling),
            device_id_type=MESH,
        )
        copy.start()
        pending.append(copy)

    owns = []
    for m in range(n):
        z_lo, t, y_lo, x, z_hi = cube(me, ())
        mine = wholes[m].at[z_lo, me["c"], t, y_lo, x, z_hi]
        own = pltpu.make_async_copy(shards[m], mine, own_sem.at[m])
        own.start()
        owns.append(own)
    ici = []

    def ici_send(m, p, phase, kind, src, dst, target):
        copy = pltpu.make_async_remote_copy(
            src_ref=src,
            dst_ref=dst,
            send_sem=send_sem.at[m, p, phase, kind],
            recv_sem=recv_sem.at[m, p, phase, kind],
            device_id=device_at(target),
            device_id_type=MESH,
        )
        copy.start()
        ici.append(copy)
        return copy

    for phase in range(3):
        first = {}
        for m in range(n):
            for p in range(3):
                axis, done = ORDERS[p][phase], ORDERS[p][:phase]
                dst = block(m, p, me, done)
                src = shards[m].at[pl.ds(16 * p, 16)] if phase == 0 else dst
                first[m, p] = [
                    ici_send(m, p, phase, kind, src, dst, moved(me, axis, step))
                    for kind, step in ((0, 1), (1, -1))
                ]
            if phase == 0:
                z_lo, t, y_lo, x, z_hi = cube(me, ())
                pair_send(shards[m], wholes[m].at[z_lo, me["c"], t, y_lo, x, z_hi], m)
        second = {}
        for m in range(n):
            for p in range(3):
                axis, done = ORDERS[p][phase], ORDERS[p][:phase]
                cols = halves(WIDTHS[m])
                out = []
                for kind, step in ((0, 1), (1, -1)):
                    first[m, p][kind].wait_recv()
                    came = moved(me, axis, -step)
                    part = block(m, p, came, done, cols[kind])
                    out.append(ici_send(m, p, phase, 2 + kind, part, part, moved(me, axis, step)))
                second[m, p] = out
                for step in (1, -1):
                    part = block(m, p, moved(me, axis, -step), done)
                    pair_send(part, part, m)
        for m in range(n):
            for p in range(3):
                axis, done = ORDERS[p][phase], ORDERS[p][:phase]
                for kind in (0, 1):
                    second[m, p][kind].wait_recv()
                part = block(m, p, moved(me, axis, 2), done)
                pair_send(part, part, m)
        if phase == 0:
            for own in owns:
                own.wait()
    for copy in ici:
        copy.wait_send()
    for copy in pending:
        copy.wait()


def gather(shards):
    n = len(WIDTHS)
    dma = pltpu.SemaphoreType.DMA
    return pl.pallas_call(
        gather_kernel,
        out_shape=[
            jax.ShapeDtypeStruct((2, 2, 2, 2, 4, 2, 48, w), jnp.bfloat16) for w in WIDTHS
        ],
        in_specs=[pl.BlockSpec(memory_space=pl.ANY)] * n,
        out_specs=[pl.BlockSpec(memory_space=pl.ANY)] * n,
        scratch_shapes=[
            dma((n, 3, 3, 4)),
            dma((n, 3, 3, 4)),
            dma((n, 28)),
            dma((n, 28)),
            dma((n,)),
        ],
        compiler_params=pltpu.CompilerParams(collective_id=0, has_side_effects=True),
        name="gather_weights",
    )(*shards)


def lead_of(whole):
    dims = []
    if "z" in whole:
        dims.append(2)
    if "y" in whole:
        dims += [2, 2]
    if "x" in whole:
        dims.append(4)
    if "z" in whole:
        dims.append(2)
    return tuple(dims)


def split_index(i, dims):
    out = []
    for size in reversed(dims):
        out.append(lax.rem(i, size))
        i = lax.div(i, size)
    return tuple(reversed(out))


def with_index(where, whole, index):
    rest = list(index)
    full = list(cube(where, whole))
    for place, value in enumerate(full):
        if isinstance(value, slice):
            full[place] = rest.pop(0)
    return tuple(full)


RS_ORDERS = tuple(tuple(reversed(order)) for order in ORDERS)
SEQUENCE = (
    (0, 0), (1, 0), (0, 1), (2, 0), (1, 1), (0, 2), (2, 1), (0, 3), (1, 2), (0, 4), (1, 3),
    (2, 2), (0, 5), (1, 4), (2, 3), (0, 6), (1, 5), (2, 4), (1, 6), (2, 5), (2, 6),
)


def reduce_scratch():
    shapes = []
    for w in WIDTHS:
        shapes.append(pltpu.VMEM((2, 2, 2, 4, 2, 48, w), jnp.bfloat16))
        cols = halves(w)
        for p in range(3):
            for phase in range(3):
                lead = lead_of(RS_ORDERS[p][phase + 1 :])
                for part in cols:
                    shapes.append(
                        pltpu.VMEM((*lead, 16, part.stop - part.start), jnp.bfloat16)
                    )
                for _ in range(2):
                    shapes.append(pltpu.VMEM((*lead, 16, w), jnp.bfloat16))
    return shapes


def reduce_kernel(*refs):
    n = len(WIDTHS)
    grads = [refs[4 * m : 4 * m + 4] for m in range(n)]
    refs = refs[4 * n :]
    sums, refs = refs[:n], refs[n:]
    landing, refs = refs[:n], refs[n:]
    held, boxes = [], {}
    for m in range(n):
        held.append(refs[0])
        refs = refs[1:]
        for p in range(3):
            for phase in range(3):
                boxes[m, p, phase] = refs[:4]
                refs = refs[4:]
    stage, send_sem, recv_sem, send_pair, recv_pair, own_sem, stage_sem = refs
    me = coordinates()
    sibling = {**me, "c": 1 - me["c"]}
    greet(me)

    def own_copy(m, z_lo, src):
        return pltpu.make_async_copy(src, held[m].at[z_lo], own_sem.at[m, z_lo])

    def pair_copy(m, z_lo, src):
        return pltpu.make_async_remote_copy(
            src_ref=src,
            dst_ref=landing[m].at[z_lo],
            send_sem=send_pair.at[m, z_lo],
            recv_sem=recv_pair.at[m, z_lo],
            device_id=device_at(sibling),
            device_id_type=MESH,
        )

    for m in range(n):
        for z_lo in range(2):
            for c in range(2):

                @pl.when(me["c"] == c)
                def _():
                    pair_copy(m, z_lo, grads[m][2 * z_lo + 1 - c]).start()
                    own_copy(m, z_lo, grads[m][2 * z_lo + c]).start()

    def stage_copy(m, i, slot):
        z_lo, t, y_lo, x = split_index(i, (2, 2, 2, 4))
        return pltpu.make_async_copy(
            landing[m].at[z_lo, t, y_lo, x],
            stage.at[slot, :, :, pl.ds(0, WIDTHS[m])],
            stage_sem.at[slot],
        )

    def add_pair(m):
        for z_lo in range(2):
            pair_copy(m, z_lo, grads[m][2 * z_lo]).wait()
            own_copy(m, z_lo, grads[m][2 * z_lo]).wait()
        stage_copy(m, 0, 0).start()

        @pl.loop(0, 32)
        def _(i):
            slot = lax.rem(i, 2)

            @pl.when(i < 31)
            def _():
                stage_copy(m, i + 1, 1 - slot).start()

            stage_copy(m, i, slot).wait()
            z_lo, t, y_lo, x = split_index(i, (2, 2, 2, 4))
            for z_hi in range(2):
                for r in range(0, 48, 16):
                    place = (z_lo, t, y_lo, x, z_hi, pl.ds(r, 16), slice(None))
                    mine = held[m][place].astype(jnp.float32)
                    other = stage[slot, z_hi, pl.ds(r, 16), pl.ds(0, WIDTHS[m])]
                    held[m][place] = to_low(mine + other.astype(jnp.float32))

    def exchange(m, p, phase, kind):
        axis, whole = RS_ORDERS[p][phase], RS_ORDERS[p][phase + 1 :]
        cols = halves(WIDTHS[m])
        step = 1 if kind % 2 == 0 else -1
        if kind < 2:
            source = moved(me, axis, 2)
            span = cols[kind]
        else:
            source = moved(me, axis, step)
            span = slice(None)
        return pltpu.make_async_remote_copy(
            src_ref=held[m].at[(*cube(source, whole), pl.ds(16 * p, 16), span)],
            dst_ref=boxes[m, p, phase][kind],
            send_sem=send_sem.at[m, p, phase, kind],
            recv_sem=recv_sem.at[m, p, phase, kind],
            device_id=device_at(moved(me, axis, step)),
            device_id_type=MESH,
        )

    def add_boxes(m, p, phase, where, span, kinds):
        whole = RS_ORDERS[p][phase + 1 :]
        dims = lead_of(whole)
        count = 1
        for size in dims:
            count *= size

        @pl.loop(0, count)
        def _(i):
            index = split_index(i, dims)
            place = (*with_index(where, whole, index), pl.ds(16 * p, 16), span)
            total = held[m][place].astype(jnp.float32)
            for kind in kinds:
                total = total + boxes[m, p, phase][kind][index].astype(jnp.float32)
            held[m][place] = to_low(total)

    def run(m, stage_number):
        if stage_number == 0:
            add_pair(m)
            for p in range(3):
                for kind in (0, 1):
                    exchange(m, p, 0, kind).start()
            return
        phase, late = divmod(stage_number - 1, 2)
        for p in range(3):
            axis = RS_ORDERS[p][phase]
            if late == 0:
                for kind, step in ((0, 1), (1, -1)):
                    exchange(m, p, phase, kind).wait_recv()
                    add_boxes(
                        m, p, phase, moved(me, axis, step), halves(WIDTHS[m])[kind], (kind,)
                    )
                    exchange(m, p, phase, 2 + kind).start()
            else:
                for kind in (2, 3):
                    exchange(m, p, phase, kind).wait_recv()
                add_boxes(m, p, phase, me, slice(None), (2, 3))
                if phase < 2:
                    for kind in (0, 1):
                        exchange(m, p, phase + 1, kind).start()
                else:
                    rows = pl.ds(16 * p, 16)
                    sums[m][rows, :] = held[m][(*cube(me, ()), rows, slice(None))]

    for m, stage_number in SEQUENCE:
        run(m, stage_number)
    for m in range(n):
        for p in range(3):
            for phase in range(3):
                for kind in range(4):
                    exchange(m, p, phase, kind).wait_send()


def reduce(grads):
    n = len(WIDTHS)
    dma = pltpu.SemaphoreType.DMA
    flat = [g.reshape(2, 2, 4, 2, 48, w) for group, w in zip(grads, WIDTHS) for g in group]
    outs = pl.pallas_call(
        reduce_kernel,
        out_shape=[jax.ShapeDtypeStruct((48, w), jnp.bfloat16) for w in WIDTHS]
        + [jax.ShapeDtypeStruct((2, 2, 2, 4, 2, 48, w), jnp.bfloat16) for w in WIDTHS],
        in_specs=[pl.BlockSpec(memory_space=pl.ANY)] * (4 * n),
        out_specs=[pl.BlockSpec(memory_space=pltpu.VMEM)] * n
        + [pl.BlockSpec(memory_space=pl.ANY)] * n,
        scratch_shapes=reduce_scratch()
        + [
            pltpu.VMEM((2, 2, 48, WIDE), jnp.bfloat16),
            dma((n, 3, 3, 4)),
            dma((n, 3, 3, 4)),
            dma((n, 2)),
            dma((n, 2)),
            dma((n, 2)),
            dma((2,)),
        ],
        compiler_params=pltpu.CompilerParams(
            collective_id=1, has_side_effects=True, vmem_limit_bytes=63 * 1024 * 1024
        ),
        name="reduce_grads",
    )(*flat)
    return outs[:n]


def normed(values, norm_gain):
    centre = values - jnp.mean(values, axis=-1, keepdims=True)
    spread = jnp.mean(centre * centre, axis=-1, keepdims=True)
    return centre * lax.rsqrt(spread + epsilon) * norm_gain


def gelu_exact(values):
    return jax.nn.gelu(values, approximate=False)


def dot(spec, left, right):
    return jnp.einsum(spec, left, right, preferred_element_type=jnp.float32)


def norm_back(residual, norm_gain, in_grad):
    unused, pullback = jax.vjp(normed, residual, norm_gain)
    return pullback(in_grad)


def attend_forward(residual, gain, weight):
    inputs = to_low(normed(residual, gain))
    projected = to_low(dot("rd,tdc->trc", inputs, weight[:, :, :1152]))
    projected = projected.reshape(2, SEQ, 3, 6, HEAD)
    q, k, v = projected[:, :, 0], projected[:, :, 1], projected[:, :, 2]
    scores = dot("tshd,tuhd->thsu", q, k) * HEAD ** (-0.5)
    peak = jnp.max(scores, axis=-1, keepdims=True)
    log_total = jnp.log(jnp.sum(jnp.exp(scores - peak), axis=-1, keepdims=True)) + peak
    probs = jnp.exp(scores - log_total)
    mixed = to_low(dot("thsu,tuhd->tshd", to_low(probs), v)).reshape(2, SEQ, 384)
    branch = dot("trh,tdh->rd", mixed, weight[:, :, 1152:HALF])
    return residual + branch, (residual, inputs, q, k, v, log_total, mixed)


def attend_backward(stream, gain, weight, saved):
    residual, inputs, q, k, v, log_total, mixed = saved
    scale = HEAD ** (-0.5)
    branch_grad = to_low(stream)
    out_grad = dot("rd,trh->tdh", branch_grad, mixed)
    mixed_grad = to_low(dot("rd,tdh->trh", branch_grad, weight[:, :, 1152:HALF]))
    mixed_grad = mixed_grad.reshape(2, SEQ, 6, HEAD)
    scores = dot("tshd,tuhd->thsu", q, k) * scale
    probs = jnp.exp(scores - log_total)
    v_grad = to_low(dot("thsu,tshd->tuhd", to_low(probs), mixed_grad))
    prob_grad = dot("tshd,tuhd->thsu", mixed_grad, v)
    score_grad = to_low(
        probs * (prob_grad - jnp.sum(probs * prob_grad, axis=-1, keepdims=True))
    )
    q_grad = to_low(dot("thsu,tuhd->tshd", score_grad, k) * scale)
    k_grad = to_low(dot("thsu,tshd->tuhd", score_grad, q) * scale)
    stacked = jnp.stack([q_grad, k_grad, v_grad], axis=2).reshape(2, SEQ, 1152)
    qkv_grad = dot("rd,trc->tdc", inputs, stacked)
    in_grad = dot("trc,tdc->rd", stacked, weight[:, :, :1152])
    residual_grad, gain_grad = norm_back(residual, gain, in_grad)
    return stream + residual_grad, gain_grad, to_low(jnp.concatenate([qkv_grad, out_grad], axis=2))


def dense_forward(residual, gain, up, down):
    inputs = to_low(normed(residual, gain))
    pre = dot("rd,tdf->trf", inputs, up[:, :, :HALF])
    act = to_low(gelu_exact(pre))
    branch = dot("trf,tdf->rd", act, down[:, :, :HALF])
    return residual + branch, (residual, inputs, pre, act)


def dense_backward(stream, gain, up, down, saved):
    residual, inputs, pre, act = saved
    branch_grad = to_low(stream)
    down_grad = dot("rd,trf->tdf", branch_grad, act)
    act_grad = dot("rd,tdf->trf", branch_grad, down[:, :, :HALF])
    unused, pullback = jax.vjp(gelu_exact, pre)
    pre_grad = to_low(pullback(act_grad)[0])
    up_grad = dot("rd,trf->tdf", inputs, pre_grad)
    in_grad = dot("trf,tdf->rd", pre_grad, up[:, :, :HALF])
    residual_grad, gain_grad = norm_back(residual, gain, in_grad)
    return stream + residual_grad, gain_grad, to_low(up_grad), to_low(down_grad)


def experts_both(residual, gain, router, up, down, routes, cotangent):
    inputs = to_low(normed(residual, gain))
    probs = jax.nn.softmax(dot("rd,de->re", inputs, router), axis=-1)
    labels = jnp.arange(4, dtype=jnp.int32)
    chosen = jnp.sum((routes[:, :, None] == labels).astype(jnp.float32), axis=1)
    combine = probs * chosen
    bg = cotangent
    branch = jnp.zeros((SEQ, D), jnp.float32)
    in_grad = jnp.zeros((SEQ, D), jnp.float32)
    combine_grad = []
    up_grads, down_grads = [], []
    for e in range(4):
        pre = dot("rd,tdf->trf", inputs, up[e])
        act = to_low(gelu_exact(pre))
        out = dot("trf,tdf->rd", act, down[e])
        gate = combine[:, e : e + 1]
        branch = branch + gate * out
        combine_grad.append(jnp.sum(out * bg.astype(jnp.float32), axis=-1))
        out_grad = to_low(gate * bg)
        down_grads.append(to_low(dot("rd,trf->tdf", out_grad, act)))
        act_grad = dot("rd,tdf->trf", out_grad, down[e])
        unused, pullback = jax.vjp(gelu_exact, pre)
        pre_grad = to_low(pullback(act_grad)[0])
        up_grads.append(to_low(dot("rd,trf->tdf", inputs, pre_grad)))
        in_grad = in_grad + dot("trf,tdf->rd", pre_grad, up[e])
    probs_grad = jnp.stack(combine_grad, axis=1) * chosen
    logit_grad = probs * (probs_grad - jnp.sum(probs * probs_grad, axis=-1, keepdims=True))
    router_grad = jnp.einsum(
        "rd,re->de", inputs.astype(jnp.float32), logit_grad, precision=precise
    )
    in_grad = in_grad + jnp.einsum(
        "re,de->rd", logit_grad, router.astype(jnp.float32), precision=precise
    )
    residual_grad, gain_grad = norm_back(residual, gain, in_grad)
    stream = cotangent.astype(jnp.float32) + residual_grad
    return to_low(residual + branch), stream, gain_grad, router_grad, up_grads, down_grads


def body(
    activations,
    attn_gain,
    qkv_weight,
    out_weight,
    ffn_gain,
    mlp_up,
    mlp_down,
    router,
    expert_up,
    expert_down,
    routes,
    cotangent,
):
    small = jnp.concatenate([attn_gain.T, ffn_gain.T, router], axis=1)
    small = jnp.pad(small, ((0, 0), (0, SMALL - 8)))
    out_t = jnp.transpose(out_weight, (0, 2, 1))
    attn = [
        jnp.concatenate([qkv_weight[b, 0], qkv_weight[b, 1], qkv_weight[b, 2], out_t[b]], axis=1)
        for b in range(2)
    ]
    sets = jnp.stack([attn[0], mlp_up, mlp_down.T, attn[1]])
    sets = jnp.concatenate(
        [
            sets,
            jnp.broadcast_to(small, (4, *small.shape)),
            expert_up,
            jnp.transpose(expert_down, (0, 2, 1)),
        ],
        axis=2,
    )
    sets = lax.all_to_all(
        sets, "fsdp", split_axis=0, concat_axis=0, tiled=True, axis_index_groups=GROUPS
    )
    sets = sets.reshape(48, WIDE + 2 * HALF)
    shards = [sets[:, :WIDE], sets[:, WIDE : WIDE + HALF], sets[:, WIDE + HALF :]]
    base, ups, downs = [
        whole.reshape(4, 2, D, w) for whole, w in zip(gather(shards), WIDTHS)
    ]
    small = base[0, 0, :, HALF : HALF + 8]
    gains = small[:, :4].astype(jnp.float32).T
    router_full = small[:, 4:8]
    half = lax.axis_index("tp")
    my_routes = lax.dynamic_slice_in_dim(routes, half * SEQ, SEQ, 0)

    residual = activations.astype(jnp.float32)
    residual, saved_first = attend_forward(residual, gains[0], base[0])
    residual, saved_dense = dense_forward(residual, gains[2], base[1], base[2])
    residual, saved_second = attend_forward(residual, gains[1], base[3])
    result, stream, ffn1, router_grad, up_grads, down_grads = experts_both(
        residual, gains[3], router_full, ups, downs, my_routes, cotangent
    )
    stream, attn1, second = attend_backward(stream, gains[1], base[3], saved_second)
    stream, ffn0, up_grad, down_grad = dense_backward(
        stream, gains[2], base[1], base[2], saved_dense
    )
    stream, attn0, first = attend_backward(stream, gains[0], base[0], saved_first)
    tail = jnp.concatenate([jnp.stack([attn0, attn1, ffn0, ffn1], axis=1), router_grad], axis=1)
    tail = to_low(jnp.pad(tail, ((0, 0), (0, SMALL - 8))))
    tail = jnp.broadcast_to(tail, (2, D, SMALL))
    blank = jnp.zeros_like(tail)
    group = [
        jnp.concatenate([first, tail], axis=2),
        jnp.concatenate([up_grad, blank], axis=2),
        jnp.concatenate([down_grad, blank], axis=2),
        jnp.concatenate([second, blank], axis=2),
    ]
    sums = reduce([group, up_grads, down_grads])
    sums = jnp.concatenate(sums, axis=1).reshape(4, 12, WIDE + 2 * HALF)
    sums = lax.all_to_all(
        sums, "fsdp", split_axis=0, concat_axis=0, tiled=True, axis_index_groups=GROUPS
    ).astype(jnp.float32)
    blocks = [sums[0, :, :HALF], sums[3, :, :HALF]]
    qkv_grad = jnp.stack(
        [jnp.stack([b[:, 384 * c : 384 * c + 384] for c in range(3)]) for b in blocks]
    )
    out_grad = jnp.stack([b[:, 1152:].T for b in blocks])
    tail = sums[0, :, HALF:WIDE]
    return (
        result,
        stream,
        tail[:, 0:2].T,
        qkv_grad,
        out_grad,
        tail[:, 2:4].T,
        sums[1, :, :HALF],
        sums[2, :, :HALF].T,
        tail[:, 4:8],
        sums[:, :, WIDE : WIDE + HALF],
        jnp.transpose(sums[:, :, WIDE + HALF :], (0, 2, 1)),
    )


def solution(mesh):
    placed = (
        P(("fsdp", "tp"), None),
        P(None, "fsdp"),
        P(None, None, "fsdp", "tp"),
        P(None, "tp", "fsdp"),
        P(None, "fsdp"),
        P("fsdp", "tp"),
        P("tp", "fsdp"),
        P("fsdp", None),
        P(None, "fsdp", "tp"),
        P(None, "tp", "fsdp"),
        P("fsdp", None),
        P(("fsdp", "tp"), None),
    )
    return jax.shard_map(
        body,
        mesh=mesh,
        in_specs=placed,
        out_specs=(
            P(("fsdp", "tp"), None),
            P(("fsdp", "tp"), None),
            P(None, "fsdp"),
            P(None, None, "fsdp", "tp"),
            P(None, "tp", "fsdp"),
            P(None, "fsdp"),
            P("fsdp", "tp"),
            P("tp", "fsdp"),
            P("fsdp", None),
            P(None, "fsdp", "tp"),
            P(None, "tp", "fsdp"),
        ),
        check_vma=False,
    )
```

time: 1720 us -> 571 us (0.33)
  blocking collectives: 935 us -> 0 us
  Pallas kernels: 0 us -> 290 us
  starting transfers between devices: 208 us -> 6.96 us
  local copies, waits for them, and re-layouts: 214 us -> 64.8 us
  waiting for transfers between devices: 166 us -> 17.7 us
  matrix products: 108 us -> 161 us
  other arithmetic: 60.1 us -> 16.2 us
    unnamed x3 -> x0, blocking collectives: 616 us -> none
    pallas_call x0 -> x2, Pallas kernels: none -> 290 us  [the longest x1 159 us: reduce(): pl.pallas_call(reduce_kernel, out_shape=[jax.ShapeDtypeStruct((48, w), jn...]
    all_gather x7 -> x0, blocking collectives: 287 us -> none  [the longest x2 161 us: fetch_attention(): lax.all_gather(out_weight[block_index], 'fsdp', axis=1, tiled=True)]
    unnamed x65 -> x0, starting transfers between devices: 166 us -> none
    unnamed x72 -> x0, waiting for transfers between devices: 76.7 us -> none
    unnamed x257 -> x219, local copies, waits for them, and re-layouts: 87.7 us -> 24.6 us
    all_gather x6 -> x0, waiting for transfers between devices: 57.5 us -> none  [the longest x1 57.5 us: body(): lax.all_gather(expert_down, 'fsdp', axis=2, tiled=True)]
    dot_general x2 -> x0, local copies, waits for them, and re-layouts: 54 us -> none  [the longest x1 30.7 us: expert_backward(): jnp.einsum('ecd,ecf->edf', slot_inputs, pre_grad, preferred_element_type=...]
  transfers between devices with their start and end apart: 81 -> 2, of which waited for: 8 -> 2; matrix products, arithmetic and copies ran while one was open for 27% -> 0% of each run, Pallas kernels for 0% -> 0%
where the time goes in v1:
time: 571 us; the launch traced here: 559 us
  Pallas kernels  290 us (51%)
  matrix products  161 us (28%)
  local copies, waits for them, and re-layouts  64.8 us (11%)
  waiting for transfers between devices  17.7 us (3%)
  other arithmetic  16.2 us (3%)
  starting transfers between devices  6.96 us (1%)
    dot_general x55, matrix products, dot(): return jnp.einsum(spec, left, right, preferred_element_type=jnp.float32)  160 us
    pallas_call x1, Pallas kernels, reduce(): pl.pallas_call(reduce_kernel, out_shape=[jax.ShapeDtypeStruct((48, w), jn...  159 us
    pallas_call x1, Pallas kernels, gather(): pl.pallas_call(gather_kernel, out_shape=[jax.ShapeDtypeStruct((2, 2, 2, 2...  131 us
    unnamed x219, local copies, waits for them, and re-layouts  24.6 us
    squeeze x1, local copies, waits for them, and re-layouts, body(): residual, saved_second = attend_forward(residual, gains[1], base[3])  13.7 us
  transfers between devices with their start and end apart: 2, of which 2 were waited for; matrix products, arithmetic and copies ran while one was open for 0% of the time, Pallas kernels for 0%

profile of v1, /device:TPU:0, one launch (start us, length us, event | category | flops | bytes accessed | tf_op | source)
XLA Modules:
  0.0 559.1 jit_solution(18260478057512487623)
XLA Ops:
  6.9 3.5 all-to-all-start
  10.9 9.2 %all-to-all-done = bf16[4,12,4736]{2,1,0:T(8,128)(2,1)S(1)} async-done(((bf16[4,12,4736]{2,1,0:T(8,128)(2,1)}), bf16[4,12,4736]{2,1,0:T(8,128)(2,1)S(1)}, u32[]{:S(2)}, u32[]{:S(2)}) %all-to-all-start) | async-done | bytes 454688 | tf_op jit(solution)/shard_map/all_to_all | solution.py:566
  21.6 130.8 %gather_weights.1 = (bf16[2,2,2,2,4,2,48,1664]{7,6,5,4,3,2,1,0:T(8,128)(2,1)}, bf16[2,2,2,2,4,2,48,1536]{7,6,5,4,3,2,1,0:T(8,128)(2,1)}, bf16[2,2,2,2,4,2,48,1536]{7,6,5,4,3,2,1,0:T(8,128)(2,1)}) custom-call(bf16[48,1664]{1,0:T(8,128)(2,1)} %slice.279.refs_0_, bf16[48,1536]{1,0:T(8,128)(2,1)} %get-tuple-element.98.refs_1_, ...), custom_call_target="tpu_custom_call" | custom-call | tf_op jit(solution)/shard_map/gather_weights/pallas_call | solution.py:174
  152.4 13.7 %slice_bitcast_fusion = (bf16[2,768,1664]{2,1,0:T(8,128)(2,1)}, bf16[2,768,1664]{2,1,0:T(8,128)(2,1)}, bf16[2,768,1664]{2,1,0:T(8,128)(2,1)}, bf16[2,768,1664]{2,1,0:T(8,128)(2,1)S(1)}) fusion(bf16[4,2,768,1664]{3,2,1,0:T(8,128)(2,1)} %bitcast.849), kind=kLoop, calls=%fused_computation | loop fusion | bytes 40894464 | tf_op jit(solution)/shard_map/squeeze | solution.py:583
  172.0 2.1 fusion.300
  174.4 10.3 %fusion.90 = (bf16[2,197,1536]{2,1,0:T(8,128)(2,1)S(1)}, f32[2,197,1536]{2,1,0:T(8,128)}, f32[2,1536,197]{1,2,0:T(8,128)}) fusion(f32[197,768]{1,0:T(8,128)S(1)} %get-tuple-element.124, f32[768]{0:T(1024)S(1)} %get-tuple-element.66, f32[197]{0:T(256)S(1)} %fusion.274, f32[197]{0:T(256)S(1)} %broadcast_multiply_fusion.2, ...), kind=kOutput, calls=%fused_computation.141 | convolution fusion | flops 969504768 | bytes 11380264 | tf_op jit(solution)/shard_map/rd,tdf->trf/dot_general | solution.py:431
  184.8 1.7 fusion.301
  192.9 2.1 fusion.302
  195.4 9.3 %fusion.74 = (bf16[2,197,1536]{2,1,0:T(8,128)(2,1)S(1)}, f32[2,197,1536]{2,1,0:T(8,128)}, f32[2,1536,197]{1,2,0:T(8,128)}) fusion(bf16[197,768]{1,0:T(8,128)(2,1)S(1)} %multiply_convert_fusion.2, bf16[4,2,768,1536]{3,2,1,0:T(8,128)(2,1)} %bitcast.947), kind=kOutput, calls=%fused_computation.113 | convolution fusion | flops 968899584 | bytes 11073024 | tf_op jit(solution)/shard_map/rd,tdf->trf/dot_general | solution.py:431
  204.6 9.3 %fusion.66 = (bf16[2,197,1536]{2,1,0:T(8,128)(2,1)S(1)}, f32[2,197,1536]{2,1,0:T(8,128)S(1)}, f32[2,1536,197]{1,2,0:T(8,128)}) fusion(bf16[197,768]{1,0:T(8,128)(2,1)S(1)} %multiply_convert_fusion.2, bf16[4,2,768,1536]{3,2,1,0:T(8,128)(2,1)} %bitcast.948), kind=kOutput, calls=%fused_computation.99 | convolution fusion | flops 968899584 | bytes 11073024 | tf_op jit(solution)/shard_map/rd,tdf->trf/dot_general | solution.py:431
  214.0 9.3 %fusion.58 = (bf16[2,197,1536]{2,1,0:T(8,128)(2,1)S(1)}, f32[2,197,1536]{2,1,0:T(8,128)S(1)}, f32[2,1536,197]{1,2,0:T(8,128)S(1)}) fusion(bf16[197,768]{1,0:T(8,128)(2,1)S(1)} %multiply_convert_fusion.2, bf16[4,2,768,1536]{3,2,1,0:T(8,128)(2,1)} %bitcast.949), kind=kOutput, calls=%fused_computation.85 | convolution fusion | flops 968899584 | bytes 11073024 | tf_op jit(solution)/shard_map/rd,tdf->trf/dot_general | solution.py:431
  223.7 9.4 %fusion.82 = (bf16[2,197,1536]{2,1,0:T(8,128)(2,1)S(1)}, f32[2,197,1536]{2,1,0:T(8,128)}, f32[2,1536,197]{1,2,0:T(8,128)}) fusion(bf16[197,768]{1,0:T(8,128)(2,1)S(1)} %multiply_convert_fusion.2, bf16[4,2,768,1536]{3,2,1,0:T(8,128)(2,1)} %bitcast.950), kind=kOutput, calls=%fused_computation.127 | convolution fusion | flops 968899584 | bytes 11073024 | tf_op jit(solution)/shard_map/rd,tdf->trf/dot_general | solution.py:431
  238.3 3.7 fusion.80
  242.0 4.4 fusion.180
  246.4 3.7 fusion.88
  250.1 4.4 fusion.187
  254.6 3.6 fusion.72
  258.1 4.4 fusion.188
  262.5 2.1 fusion.64
  264.6 4.4 fusion.189
  269.1 2.7 fusion.221
  274.7 2.4 fusion.201
  283.8 2.0 multiply_reduce_fusion.6
  287.7 2.4 fusion.96
  290.1 2.3 multiply_reduce_fusion.5
  293.7 2.4 fusion.202
  305.1 3.0 convolution_convert_fusion.9
  308.1 3.7 convert_bitcast_fusion.1
  311.8 3.6 convert_bitcast_fusion
  316.7 3.1 fusion.24
  319.8 3.8 convolution_convert_fusion.7
  323.6 3.6 convolution_convert_fusion.6
  327.2 3.7 convolution_convert_fusion.5
  330.9 3.6 convolution_convert_fusion.4
  334.5 3.7 convolution_convert_fusion.3
  338.2 3.7 convolution_convert_fusion.2
  341.9 3.7 convolution_convert_fusion.1
  345.7 3.6 convolution_convert_fusion
  351.0 1.8 copy.151
  352.7 5.1 concatenate.52
  357.9 2.9 concatenate.53
  361.6 2.5 pad_maximum_fusion.1
  364.0 6.6 %copy.193 = bf16[2,768,1536]{2,1,0:T(8,128)(2,1)} copy(bf16[2,768,1536]{1,2,0:T(8,128)(2,1)} %pad_maximum_fusion.1) | data formatting | bytes 9437184
  370.7 5.1 concatenate.55.clone
  375.8 2.8 pad_maximum_fusion.refs_0_
  378.6 158.7 %reduce_grads.1 = (bf16[48,1664]{1,0:T(8,128)(2,1)}, bf16[48,1536]{1,0:T(8,128)(2,1)}, bf16[48,1536]{1,0:T(8,128)(2,1)}, bf16[2,2,2,4,2,48,1664]{6,5,4,3,2,1,0:T...) custom-call(bf16[2,2,4,2,48,1664]{5,4,3,2,1,0:T(8,128)(2,1)} %pad_maximum_fusion.re, ...), custom_call_target="tpu_custom_call" | custom-call | tf_op jit(solution)/shard_map/reduce_grads/pallas_call | solution.py:395
  539.5 3.5 all-to-all-start.1
  544.1 8.6 %all-to-all-done.1 = bf16[4,12,4736]{2,1,0:T(8,128)(2,1)S(1)} async-done(((bf16[4,12,4736]{2,1,0:T(8,128)(2,1)}), bf16[4,12,4736]{2,1,0:T(8,128)(2,1)S(1)}, u32[]{:S(2)}, u32[]{:S(2)}) %all-to-all-start.1) | async-done | bytes 454688 | tf_op jit(solution)/shard_map/all_to_all | solution.py:604
  (334 shorter events, 60.9 us)
Async XLA Ops:
  0.6 10.1 %copy-start = (s32[394,2]{0,1:T(2,128)S(1)}, s32[394,2]{0,1:T(2,128)}, u32[]{:S(2)}) copy-start(s32[394,2]{0,1:T(2,128)} %param.22) | copy-start | bytes 9460
  0.7 9.7 %copy-start.15 = (bf16[197,768]{1,0:T(8,128)(2,1)S(1)}, bf16[197,768]{1,0:T(8,128)(2,1)}, u32[]{:S(2)}) copy-start(bf16[197,768]{1,0:T(8,128)(2,1)} %param.12) | copy-start | bytes 907780
  6.9 13.2 %all-to-all-start = ((bf16[4,12,4736]{2,1,0:T(8,128)(2,1)}), bf16[4,12,4736]{2,1,0:T(8,128)(2,1)S(1)}, u32[]{:S(2)}, u32[]{:S(2)}) async-start(bf16[4,12,4736]{2,1,0:T(8,128)(2,1)} %pad_maximum_fusion.4), calls=%async_computation | async-start | bytes 1212416 | tf_op jit(solution)/shard_map/all_to_all | solution.py:566
  10.5 157.6 %copy-start.61 = (f32[197]{0:T(256)}, f32[197]{0:T(256)S(1)}, u32[]{:S(2)}) copy-start(f32[197]{0:T(256)S(1)} %broadcast_multiply_fusion.3) | copy-start | bytes 2368
  10.8 155.3 %copy-start.65 = (f32[197]{0:T(256)}, f32[197]{0:T(256)S(1)}, u32[]{:S(2)}) copy-start(f32[197]{0:T(256)S(1)} %fusion.215) | copy-start | bytes 2368
  10.9 157.2 %copy-start.63 = (f32[197]{0:T(256)}, f32[197]{0:T(256)S(1)}, u32[]{:S(2)}) copy-start(f32[197]{0:T(256)S(1)} %fusion.273) | copy-start | bytes 2368
  172.0 12.8 %slice-start.10 = ((s8[5111808]{0:T(1024)(128)(4,1)}), s8[4194304]{0:T(1024)(128)(4,1)S(1)}, s32[]{:S(2)}) async-start(s8[5111808]{0:T(1024)(128)(4,1)} %bitcast.885), calls=%async_computation.12 | async-start | bytes 8388608
  172.0 14.7 %slice-start.2 = ((s8[5111808]{0:T(1024)(128)(4,1)}), s8[4194304]{0:T(1024)(128)(4,1)S(1)}, s32[]{:S(2)}) async-start(s8[5111808]{0:T(1024)(128)(4,1)} %bitcast.877), calls=%async_computation.4 | async-start | bytes 8388608
  174.1 10.6 %copy-start.24 = (f32[197,768]{1,0:T(8,128)}, f32[197,768]{1,0:T(8,128)S(1)}, u32[]{:S(2)}) copy-start(f32[197,768]{1,0:T(8,128)S(1)} %get-tuple-element.124) | copy-start | bytes 1815556
  174.3 10.4 %copy-start.67 = (f32[197]{0:T(256)}, f32[197]{0:T(256)S(1)}, u32[]{:S(2)}) copy-start(f32[197]{0:T(256)S(1)} %multiply_reduce_fusion.12) | copy-start | bytes 2368
  174.4 10.4 %slice-start.11 = ((s8[5111808]{0:T(1024)(128)(4,1)}), s8[917504]{0:T(1024)(128)(4,1)S(1)}, s32[]{:S(2)}) async-start(s8[5111808]{0:T(1024)(128)(4,1)} %bitcast.885), calls=%async_computation.13 | async-start | bytes 1835008
  174.4 12.4 %slice-start.3 = ((s8[5111808]{0:T(1024)(128)(4,1)}), s8[917504]{0:T(1024)(128)(4,1)S(1)}, s32[]{:S(2)}) async-start(s8[5111808]{0:T(1024)(128)(4,1)} %bitcast.877), calls=%async_computation.5 | async-start | bytes 1835008
  186.5 6.4 %copy-start.12 = (f32[197,768]{1,0:T(8,128)}, f32[197,768]{1,0:T(8,128)S(1)}, u32[]{:S(2)}) copy-start(f32[197,768]{1,0:T(8,128)S(1)} %get-tuple-element.127) | copy-start | bytes 1815556
  204.6 28.5 %copy-start.32 = (bf16[2,197,1536]{2,1,0:T(8,128)(2,1)}, bf16[2,197,1536]{2,1,0:T(8,128)(2,1)S(1)}, u32[]{:S(2)}) copy-start(bf16[2,197,1536]{2,1,0:T(8,128)(2,1)S(1)} %get-tuple-element.80) | copy-start | bytes 3631108
  214.0 20.9 %copy-start.34 = (bf16[2,197,1536]{2,1,0:T(8,128)(2,1)}, bf16[2,197,1536]{2,1,0:T(8,128)(2,1)S(1)}, u32[]{:S(2)}) copy-start(bf16[2,197,1536]{2,1,0:T(8,128)(2,1)S(1)} %get-tuple-element.82) | copy-start | bytes 3631108
  214.0 19.2 %slice-start.14 = ((s8[18874368]{0:T(1024)(128)(4,1)}), s8[4194304]{0:T(1024)(128)(4,1)S(1)}, s32[]{:S(2)}) async-start(s8[18874368]{0:T(1024)(128)(4,1)} %bitcast.937), calls=%async_computation.16 | async-start | bytes 8388608
  214.0 19.2 %slice-start.15 = ((s8[18874368]{0:T(1024)(128)(4,1)}), s8[4194304]{0:T(1024)(128)(4,1)S(1)}, s32[]{:S(2)}) async-start(s8[18874368]{0:T(1024)(128)(4,1)} %bitcast.937), calls=%async_computation.17 | async-start | bytes 8388608
  214.0 19.2 %slice-start.16 = ((s8[18874368]{0:T(1024)(128)(4,1)}), s8[4194304]{0:T(1024)(128)(4,1)S(1)}, s32[]{:S(2)}) async-start(s8[18874368]{0:T(1024)(128)(4,1)} %bitcast.937), calls=%async_computation.18 | async-start | bytes 8388608
  223.3 13.2 %copy-start.36 = (bf16[2,197,1536]{2,1,0:T(8,128)(2,1)}, bf16[2,197,1536]{2,1,0:T(8,128)(2,1)S(1)}, u32[]{:S(2)}) copy-start(bf16[2,197,1536]{2,1,0:T(8,128)(2,1)S(1)} %get-tuple-element.84) | copy-start | bytes 3631108
  223.7 9.5 %slice-start.17 = ((s8[18874368]{0:T(1024)(128)(4,1)}), s8[4194304]{0:T(1024)(128)(4,1)S(1)}, s32[]{:S(2)}) async-start(s8[18874368]{0:T(1024)(128)(4,1)} %bitcast.937), calls=%async_computation.19 | async-start | bytes 8388608
  223.7 9.5 %slice-start.18 = ((s8[18874368]{0:T(1024)(128)(4,1)}), s8[2097152]{0:T(1024)(128)(4,1)S(1)}, s32[]{:S(2)}) async-start(s8[18874368]{0:T(1024)(128)(4,1)} %bitcast.937), calls=%async_computation.20 | async-start | bytes 4194304
  233.1 35.9 %copy-start.38 = (bf16[2,197,1536]{2,1,0:T(8,128)(2,1)}, bf16[2,197,1536]{2,1,0:T(8,128)(2,1)S(1)}, u32[]{:S(2)}) copy-start(bf16[2,197,1536]{2,1,0:T(8,128)(2,1)S(1)} %get-tuple-element.78) | copy-start | bytes 3631108
  238.2 30.9 %copy-start.69 = (f32[197,1]{0,1:T(1,128)}, f32[197,1]{0,1:T(1,128)S(1)}, u32[]{:S(2)}) copy-start(f32[197,1]{0,1:T(1,128)S(1)} %get-tuple-element.118) | copy-start | bytes 2368
  238.2 30.9 %copy-start.71 = (f32[197,1]{0,1:T(1,128)}, f32[197,1]{0,1:T(1,128)S(1)}, u32[]{:S(2)}) copy-start(f32[197,1]{0,1:T(1,128)S(1)} %get-tuple-element.119) | copy-start | bytes 2368
  238.2 30.9 %copy-start.73 = (f32[197,1]{0,1:T(1,128)}, f32[197,1]{0,1:T(1,128)S(1)}, u32[]{:S(2)}) copy-start(f32[197,1]{0,1:T(1,128)S(1)} %get-tuple-element.120) | copy-start | bytes 2368
  238.2 30.9 %copy-start.75 = (f32[197,1]{0,1:T(1,128)}, f32[197,1]{0,1:T(1,128)S(1)}, u32[]{:S(2)}) copy-start(f32[197,1]{0,1:T(1,128)S(1)} %get-tuple-element.117) | copy-start | bytes 2368
  242.0 4.4 copy-start.40
  250.1 4.4 copy-start.42
  258.1 4.4 copy-start.44
  264.6 4.4 copy-start.46
  282.2 4.2 slice-start.12
  283.8 6.3 %slice-start.8 = ((s8[5111808]{0:T(1024)(128)(4,1)}), s8[917504]{0:T(1024)(128)(4,1)S(1)}, s32[]{:S(2)}) async-start(s8[5111808]{0:T(1024)(128)(4,1)} %bitcast.883), calls=%async_computation.10 | async-start | bytes 1835008
  286.3 6.4 %copy-start.22 = (f32[197,768]{1,0:T(8,128)}, f32[197,768]{1,0:T(8,128)S(1)}, u32[]{:S(2)}) copy-start(f32[197,768]{1,0:T(8,128)S(1)} %add_add_fusion.6) | copy-start | bytes 1815556
  292.7 4.6 copy-start.3
  292.7 4.6 copy-start.58
  305.1 44.2 %copy-start.50 = (f32[197,768]{1,0:T(8,128)}, f32[197,768]{1,0:T(8,128)S(1)}, u32[]{:S(2)}) copy-start(f32[197,768]{1,0:T(8,128)S(1)} %get-tuple-element.146) | copy-start | bytes 1815556
  311.8 4.1 copy-start.14
  319.8 3.8 copy-start.41
  345.7 4.3 copy-start.77
  345.7 4.3 copy-start.78
  350.9 6.9 %slice-start = ((s8[4718592]{0:T(1024)(128)(4,1)}), s8[524288]{0:T(1024)(128)(4,1)S(1)}, s32[]{:S(2)}) async-start(s8[4718592]{0:T(1024)(128)(4,1)} %bitcast.862), calls=%async_computation.2 | async-start | bytes 1048576
  352.7 5.1 slice-start.1
  370.7 5.1 copy-start.56
  370.7 5.2 copy-start.4
  537.4 5.7 %copy-start.21 = (f32[197,768]{1,0:T(8,128)S(1)}, f32[197,768]{1,0:T(8,128)}, u32[]{:S(2)}) copy-start(f32[197,768]{1,0:T(8,128)} %copy-done.19) | copy-start | bytes 1815556
  537.4 5.7 %copy-start.51 = (f32[197,768]{1,0:T(8,128)S(1)}, f32[197,768]{1,0:T(8,128)}, u32[]{:S(2)}) copy-start(f32[197,768]{1,0:T(8,128)} %copy-done.50) | copy-start | bytes 1815556
  539.5 13.2 %all-to-all-start.1 = ((bf16[4,12,4736]{2,1,0:T(8,128)(2,1)}), bf16[4,12,4736]{2,1,0:T(8,128)(2,1)S(1)}, u32[]{:S(2)}, u32[]{:S(2)}) async-start(bf16[4,12,4736]{2,1,0:T(8,128)(2,1)} %reshape.261), calls=%async_computation.1 | async-start | bytes 1212416 | tf_op jit(solution)/shard_map/all_to_all | solution.py:604
  552.8 6.1 %copy-start.1 = (s32[394,2]{0,1:T(2,128)S(1)}, s32[394,2]{0,1:T(2,128)}, u32[]{:S(2)}) copy-start(s32[394,2]{0,1:T(2,128)} %param.22) | copy-start | bytes 9460
  (54 other events, 133.2 us)
